TPU v7x, 32 devices: a whole 2x2x4 slice. The times are simulated.
32 devices in a mesh: dp: 8 (over y, x, core), expert: 4 (over z).
Axes of the slice: x: 2, y: 2, z: 4, core: 2. Of those that a mesh axis runs over, the one named last changes fastest.
Arguments:
- tokens: bfloat16 [4096, 1024], P(('dp', 'expert')), may hold values from -6 to 6
- routing: int32 [4096, 2], P(('dp', 'expert')), may hold values from 0 to 3, as said below
- combine: float32 [4096, 2], P(('dp', 'expert')), may hold values from 0.1 to 1
- upstream: bfloat16 [4096, 1024], P(('dp', 'expert')), may hold values from -6 to 6
- gate_weight: bfloat16 [4, 1024, 384], P('expert', 'dp'), may hold values from -0.1875 to 0.1875
- up_weight: bfloat16 [4, 1024, 384], P('expert', 'dp'), may hold values from -0.1875 to 0.1875
- down_weight: bfloat16 [4, 1024, 384], P('expert', 'dp'), may hold values from -0.3125 to 0.3125
Outputs:
- layer_output: bfloat16 [4096, 1024], P(('dp', 'expert'))
- token_grad: bfloat16 [4096, 1024], P(('dp', 'expert'))
- combine_grad: float32 [4096, 2], P(('dp', 'expert'))
- gate_grad: float32 [4, 1024, 384], P('expert', 'dp')
- up_grad: float32 [4, 1024, 384], P('expert', 'dp')
Inputs may be any that keep to these rules, and one draw needn't show every extreme that they name: `routing`: each row names 2 different experts. The rows fall into blocks of 128 (the rows of one device), and 4 consecutive blocks form a data group. In each data group one expert, the group's hot expert, is named by exactly 96 rows of every block of the group; a second expert of the group is named by exactly 64 rows of every block of the group; every other expert is named by at most 64 rows of a block.
All inputs are finite; a program needn't handle non-finite values.
Results may differ from a plain program's by a relative error of at most 0.0065.
Values may be sent and summed in bfloat16 or wider, within the bound.
A program may use at most 64 MiB of HBM per device.

v0:
```python
import jax
import jax.numpy as jnp
from jax import lax
from jax.sharding import PartitionSpec as P


def expert_forward(input_rows, gate_full, up_full, down_full):
    gate_pre = jnp.dot(input_rows, gate_full, preferred_element_type=jnp.float32)
    up_pre = jnp.dot(input_rows, up_full, preferred_element_type=jnp.float32)
    hidden = (jax.nn.silu(gate_pre) * up_pre).astype(jnp.bfloat16)
    results = lax.dot_general(
        hidden, down_full, (((1,), (1,)), ((), ())), preferred_element_type=jnp.float32
    )
    return (results.astype(jnp.bfloat16), gate_pre, up_pre)


def expert_backward(cotangent, gate_pre, up_pre, stacked, down_full):
    hidden_grad = jnp.dot(cotangent, down_full, preferred_element_type=jnp.float32)
    sigmoid_value = jax.nn.sigmoid(gate_pre)
    gate_delta = (
        hidden_grad * up_pre * sigmoid_value * (1.0 + gate_pre * (1.0 - sigmoid_value))
    ).astype(jnp.bfloat16)
    up_delta = (hidden_grad * jax.nn.silu(gate_pre)).astype(jnp.bfloat16)
    deltas = jnp.concatenate([gate_delta, up_delta], axis=1)
    input_grads = lax.dot_general(
        deltas, stacked, (((1,), (1,)), ((), ())), preferred_element_type=jnp.float32
    )
    return (input_grads.astype(jnp.bfloat16), deltas)


def trade_rows(buffer):
    return lax.all_to_all(buffer, "expert", split_axis=0, concat_axis=0, tiled=True)


def pick_slots(routing, expert_total):
    flat_ids = routing.reshape(-1)
    match_table = (flat_ids[:, None] == jnp.arange(expert_total, dtype=jnp.int32)[None, :]).astype(
        jnp.int32
    )
    position = jnp.sum((jnp.cumsum(match_table, axis=0) - 1) * match_table, axis=1)
    expert_loads = jnp.sum(match_table, axis=0)
    return (flat_ids, position, expert_loads)


def reduce_grads(arrived, deltas):
    piece = lax.dot_general(
        arrived, deltas, (((0,), (0,)), ((), ())), preferred_element_type=jnp.float32
    )
    return lax.psum_scatter(piece, "dp", scatter_dimension=0, tiled=True)


def shards(tokens, routing, combine, upstream, gate_weight, up_weight, down_weight):
    tok_count = tokens.shape[0]
    top_count = routing.shape[1]
    pick_total = tok_count * top_count
    feature_total = tokens.shape[1]
    hidden_total = gate_weight.shape[2]
    expert_total = lax.axis_size("expert")
    group_total = lax.axis_size("dp")
    capacity = max(tok_count // 2, top_count * tok_count // expert_total + tok_count // 4)
    gate_full, up_full, down_full = (
        lax.all_gather(gate_weight, "dp", axis=1, tiled=True),
        lax.all_gather(up_weight, "dp", axis=1, tiled=True),
        lax.all_gather(down_weight, "dp", axis=1, tiled=True),
    )
    gate_full = gate_full[0]
    up_full = up_full[0]
    down_full = down_full[0]
    stacked = jnp.concatenate([gate_full, up_full], axis=1)
    flat_ids, position, expert_loads = pick_slots(routing, expert_total)
    pick_index = jnp.arange(pick_total, dtype=jnp.int32)
    owners = pick_index // top_count
    upstream_wide = upstream.astype(jnp.float32)
    pick_cotangent = (
        (combine[:, :, None] * upstream_wide[:, None, :])
        .reshape(pick_total, feature_total)
        .astype(jnp.bfloat16)
    )
    slot_index = jnp.where(flat_ids >= 0, flat_ids * capacity + position, expert_total * capacity)
    token_source = (
        jnp.full((expert_total * capacity,), tok_count, jnp.int32)
        .at[slot_index]
        .set(owners, mode="drop")
    )
    pick_source = (
        jnp.full((expert_total * capacity,), pick_total, jnp.int32)
        .at[slot_index]
        .set(pick_index, mode="drop")
    )
    sending = jnp.take(tokens, token_source, axis=0, mode="fill", fill_value=0)
    arrived = trade_rows(sending.reshape(expert_total, capacity, feature_total)).reshape(
        expert_total * capacity, feature_total
    )
    results, gate_pre, up_pre = expert_forward(arrived, gate_full, up_full, down_full)
    returned = trade_rows(results.reshape(expert_total, capacity, feature_total)).reshape(
        expert_total * capacity, feature_total
    )
    pick_rows = jnp.take(returned, slot_index, axis=0, mode="fill", fill_value=0)
    cot_send = jnp.take(pick_cotangent, pick_source, axis=0, mode="fill", fill_value=0)
    cot_arrived = trade_rows(cot_send.reshape(expert_total, capacity, feature_total)).reshape(
        expert_total * capacity, feature_total
    )
    input_grads, deltas = expert_backward(cot_arrived, gate_pre, up_pre, stacked, down_full)
    grads_back = trade_rows(input_grads.reshape(expert_total, capacity, feature_total)).reshape(
        expert_total * capacity, feature_total
    )
    pick_grads = jnp.take(grads_back, slot_index, axis=0, mode="fill", fill_value=0)
    pick_rows, pick_grads, arrived, deltas = (pick_rows, pick_grads, arrived, deltas)
    summed = reduce_grads(arrived, deltas) / group_total
    gate_grad = summed[:, :hidden_total][None]
    up_grad = summed[:, hidden_total:][None]
    pick_wide = pick_rows.reshape(tok_count, top_count, feature_total).astype(jnp.float32)
    layer_output = jnp.sum(combine[:, :, None] * pick_wide, axis=1).astype(jnp.bfloat16)
    combine_grad = jnp.sum(upstream_wide[:, None, :] * pick_wide, axis=2)
    token_grad = jnp.sum(
        pick_grads.reshape(tok_count, top_count, feature_total).astype(jnp.float32), axis=1
    ).astype(jnp.bfloat16)
    return (layer_output, token_grad, combine_grad, gate_grad, up_grad)


def solution(mesh):
    placed = (
        P(("dp", "expert"), None),
        P(("dp", "expert"), None),
        P(("dp", "expert"), None),
        P(("dp", "expert"), None),
        P("expert", "dp", None),
        P("expert", "dp", None),
        P("expert", "dp", None),
    )
    return jax.shard_map(
        shards,
        mesh=mesh,
        in_specs=placed,
        out_specs=(
            P(("dp", "expert"), None),
            P(("dp", "expert"), None),
            P(("dp", "expert"), None),
            P("expert", "dp", None),
            P("expert", "dp", None),
        ),
        check_vma=False,
    )
```

profile of v0, /device:TPU:0, one launch (start us, length us, event | category | flops | bytes accessed | tf_op | source)
XLA Modules:
  0.0 164.7 jit_solution(4844647668749269878)
XLA Ops:
  7.2 0.0 copy-start
  7.2 0.7 broadcast_compare_fusion
  7.9 0.7 broadcast_multiply_fusion.1
  8.6 0.8 copy.16
  9.4 0.1 eq.29
  9.5 0.1 eq.25
  9.7 0.1 copy.20
  9.8 0.1 ge.35
  10.0 0.1 copy.21
  10.1 0.1 mul.82
  10.2 1.2 reduce-window.6
  11.5 0.1 slice.24
  11.5 0.1 copy.18
  11.7 0.1 copy.19
  11.8 0.1 add_bitcast_fusion
  11.9 1.4 scatter_custom_fusion
  13.3 0.1 broadcast_in_dim.62
  13.4 2.1 %gather_fusion = bf16[384,1024]{1,0:T(8,128)(2,1)S(1)} fusion(bf16[128,1024]{1,0:T(8,128)(2,1)S(1)} %copy-done, s32[1024]{0:T(1024)S(1)} %pad_clamp_fusion.2), kind=kCustom, calls=%fused_computation.2 | custom fusion | bytes 1574400 | tf_op jit(solution)/shard_map/jit(_take)/gather | solution.py:90
  15.5 0.0 copy-start.14
  15.5 1.0 broadcast_select_fusion.1
  16.5 6.4 %all-to-all-start = ((bf16[4,96,1024]{2,1,0:T(8,128)(2,1)}), bf16[4,96,1024]{2,1,0:T(8,128)(2,1)S(1)}, u32[]{:S(2)}, u32[]{:S(2)}) async-start(bf16[4,96,1024]{2,1,0:T(8,128)(2,1)} %broadcast_select_fusion.1), calls=%async_computation | async-start | bytes 1572864 | tf_op jit(solution)/shard_map/all_to_all | solution.py:32
  23.0 10.4 %all_gather.10 = bf16[1,1024,384]{2,1,0:T(8,128)(2,1)S(1)} all-gather(bf16[1,128,384]{2,1,0:T(8,128)(2,1)S(1)} %copy-done.14), channel_id=1, replica_groups=mesh['dp'=8,'expert'=4] {'dp'}, dimensions={1}, use_global_device_ids=true | all-gather | bytes 884736 | tf_op jit(solution)/shard_map/all_gather | solution.py:63
  33.4 10.4 %all_gather.9 = bf16[1,1024,384]{2,1,0:T(8,128)(2,1)S(1)} all-gather(bf16[1,128,384]{2,1,0:T(8,128)(2,1)S(1)} %copy-done.15), channel_id=1, replica_groups=mesh['dp'=8,'expert'=4] {'dp'}, dimensions={1}, use_global_device_ids=true | all-gather | bytes 884736 | tf_op jit(solution)/shard_map/all_gather | solution.py:62
  43.8 9.4 %all_gather.11 = bf16[1,1024,384]{2,1,0:T(8,128)(2,1)S(1)} all-gather(bf16[1,128,384]{2,1,0:T(8,128)(2,1)S(1)} %copy-done.16), channel_id=1, replica_groups=mesh['dp'=8,'expert'=4] {'dp'}, dimensions={1}, use_global_device_ids=true | all-gather | bytes 884736 | tf_op jit(solution)/shard_map/all_gather | solution.py:64
  53.2 0.0 all-to-all-done
  53.2 0.6 fusion.23
  53.8 0.0 copy-done.2
  53.8 0.0 copy-start.9
  53.8 0.6 fusion.21
  54.5 1.5 convolution_convert_fusion
  56.0 5.2 %all-to-all-start.1 = ((bf16[4,96,1024]{2,1,0:T(8,128)(2,1)}), bf16[4,96,1024]{2,1,0:T(8,128)(2,1)S(1)}, u32[]{:S(2)}, u32[]{:S(2)}) async-start(bf16[4,96,1024]{2,1,0:T(8,128)(2,1)} %bitcast.55), calls=%async_computation.1 | async-start | bytes 1572864 | tf_op jit(solution)/shard_map/all_to_all | solution.py:32
  61.3 0.3 mul.91
  61.6 1.7 %mul.92 = f32[256,1024]{1,0:T(8,128)} reshape(f32[128,2,1024]{2,1,0:T(2,128)S(1)} %mul.91) | data formatting | bytes 2097152 | tf_op jit(solution)/shard_map/mul | solution.py:75
  63.2 0.1 copy.15
  63.4 0.1 mul.89
  63.5 1.4 scatter_custom_fusion.1
  64.9 0.1 broadcast_in_dim.68
  65.1 16.8 %all-to-all-done.1 = bf16[4,96,1024]{2,1,0:T(8,128)(2,1)S(1)} async-done(((bf16[4,96,1024]{2,1,0:T(8,128)(2,1)}), bf16[4,96,1024]{2,1,0:T(8,128)(2,1)S(1)}, u32[]{:S(2)}, u32[]{:S(2)}) %all-to-all-start.1) | async-done | bytes 786464 | tf_op jit(solution)/shard_map/all_to_all | solution.py:32
  81.9 1.2 gather_fusion.2
  83.1 0.1 copy-done.1
  83.1 0.3 multiply_reduce_fusion
  83.4 2.1 %gather_fusion.1 = bf16[384,1024]{1,0:T(8,128)(2,1)S(1)} fusion(bf16[256,1024]{1,0:T(8,128)(2,1)S(1)} %get-tuple-element.16, s32[1024]{0:T(1024)S(1)} %pad_clamp_fusion), kind=kCustom, calls=%fused_computation.3 | custom fusion | bytes 1574400 | tf_op jit(solution)/shard_map/jit(_take)/gather | solution.py:99
  85.6 0.1 broadcast_select_fusion
  85.7 22.3 %all_to_all.20 = bf16[4,96,1024]{2,1,0:T(8,128)(2,1)S(1)} all-to-all(bf16[4,96,1024]{2,1,0:T(8,128)(2,1)S(1)} %broadcast_select_fusion), channel_id=1, replica_groups=mesh['dp'=8,'expert'=4] {'expert'}, dimensions={0} | all-to-all | bytes 1572864 | tf_op jit(solution)/shard_map/all_to_all | solution.py:32
  108.0 0.8 multiply_convert_fusion.2
  108.8 2.7 %fusion.11 = f32[1024,768]{1,0:T(8,128)} fusion(bf16[384,1024]{1,0:T(8,128)(2,1)S(1)} %bitcast.50, bf16[384,384]{0,1:T(8,128)(2,1)S(1)} %get-tuple-element.14, bf16[384,384]{0,1:T(8,128)(2,1)S(1)} %get-tuple-element.13), kind=kOutput, calls=%fused_computation.28 | convolution fusion | flops 605159424 | bytes 4521984 | tf_op jit(solution)/shard_map/dot_general | solution.py:46
  111.4 0.0 reduce-scatter.2.cloned.1.call-update
  111.5 1.1 copy-done.3
  112.6 0.2 copy-done.5
  112.8 1.7 %fusion.4 = bf16[384,1024]{1,0:T(8,128)(2,1)} fusion(bf16[1024,384]{1,0:T(8,128)(2,1)S(1)} %bitcast.51, bf16[1024,384]{1,0:T(8,128)(2,1)S(1)} %bitcast.52, bf16[384,384]{0,1:T(8,128)(2,1)S(1)} %get-tuple-element.14, bf16[384,384]{0,1:T(8,128)(2,1)S(1)} %get-tuple-element.13), kind=kOutput, calls=%fused_computation.10 | convolution fusion | flops 608698368 | bytes 2949120 | tf_op jit(solution)/shard_map/dot_general | solution.py:25
  114.5 3.5 %all-to-all-start.3 = ((bf16[4,96,1024]{2,1,0:T(8,128)(2,1)}), bf16[4,96,1024]{2,1,0:T(8,128)(2,1)S(1)}, u32[]{:S(2)}, u32[]{:S(2)}) async-start(bf16[4,96,1024]{2,1,0:T(8,128)(2,1)} %bitcast.13), calls=%async_computation.3 | async-start | bytes 1572864 | tf_op jit(solution)/shard_map/all_to_all | solution.py:32
  118.0 0.1 reduce_sum.48
  118.2 0.6 copy.23
  118.8 18.4 %all-to-all-done.3 = bf16[4,96,1024]{2,1,0:T(8,128)(2,1)S(1)} async-done(((bf16[4,96,1024]{2,1,0:T(8,128)(2,1)}), bf16[4,96,1024]{2,1,0:T(8,128)(2,1)S(1)}, u32[]{:S(2)}, u32[]{:S(2)}) %all-to-all-start.3) | async-done | bytes 786464 | tf_op jit(solution)/shard_map/all_to_all | solution.py:32
  137.2 1.2 gather_fusion.3
  138.3 1.0 broadcast_select_fusion.2
  139.3 0.6 reshape.140
  139.9 0.4 copy-done.6
  140.4 0.2 reshape.139
  140.6 2.1 %reduce_sum.46 = bf16[128,1024]{1,0:T(8,128)(2,1)} reduce(bf16[128,2,1024]{2,1,0:T(2,128)(2,1)S(1)} %reshape.139, bf16[]{:T(256)} %constant.75.clone.1), dimensions={1}, to_apply=%region_6.8 | reduce | flops 131072 | bytes 786434 | tf_op jit(solution)/shard_map/reduce_sum | solution.py:115
  142.6 2.1 %multiply_reduce_fusion.1 = bf16[128,1024]{1,0:T(8,128)(2,1)} fusion(f32[128,2,1024]{2,1,0:T(2,128)S(1)} %reshape.140, f32[128,2]{1,0:T(8,128)S(1)} %copy.15), kind=kLoop, calls=%fused_computation.14 | loop fusion | flops 393216 | bytes 1311744 | tf_op jit(solution)/shard_map/reduce_sum | solution.py:113
  144.7 11.3 %reduce-scatter.2.cloned.1.call-done = f32[128,768]{1,0:T(8,128)} async-done(((f32[1024,768]{1,0:T(8,128)}), f32[128,768]{1,0:T(8,128)}) %reduce-scatter.2.cloned.1.call-update) | async-done | bytes 393232 | tf_op jit(solution)/shard_map/reduce_scatter | solution.py:49
  156.0 1.0 broadcast_multiply_fusion
  157.1 0.8 slice_bitcast_fusion
  (44 shorter events, 0.2 us)
Async XLA Ops:
  7.2 6.2 %copy-start = (bf16[128,1024]{1,0:T(8,128)(2,1)S(1)}, bf16[128,1024]{1,0:T(8,128)(2,1)}, u32[]{:S(2)}) copy-start(bf16[128,1024]{1,0:T(8,128)(2,1)} %param.9) | copy-start | bytes 786436
  15.5 7.5 %copy-start.14 = (bf16[1,128,384]{2,1,0:T(8,128)(2,1)S(1)}, bf16[1,128,384]{2,1,0:T(8,128)(2,1)}, u32[]{:S(2)}) copy-start(bf16[1,128,384]{2,1,0:T(8,128)(2,1)} %param.14) | copy-start | bytes 294916
  16.5 16.9 %copy-start.15 = (bf16[1,128,384]{2,1,0:T(8,128)(2,1)S(1)}, bf16[1,128,384]{2,1,0:T(8,128)(2,1)}, u32[]{:S(2)}) copy-start(bf16[1,128,384]{2,1,0:T(8,128)(2,1)} %param.13) | copy-start | bytes 294916
  16.5 27.2 %copy-start.16 = (bf16[1,128,384]{2,1,0:T(8,128)(2,1)S(1)}, bf16[1,128,384]{2,1,0:T(8,128)(2,1)}, u32[]{:S(2)}) copy-start(bf16[1,128,384]{2,1,0:T(8,128)(2,1)} %param.15) | copy-start | bytes 294916
  16.5 36.7 %all-to-all-start = ((bf16[4,96,1024]{2,1,0:T(8,128)(2,1)}), bf16[4,96,1024]{2,1,0:T(8,128)(2,1)S(1)}, u32[]{:S(2)}, u32[]{:S(2)}) async-start(bf16[4,96,1024]{2,1,0:T(8,128)(2,1)} %broadcast_select_fusion.1), calls=%async_computation | async-start | bytes 1572864 | tf_op jit(solution)/shard_map/all_to_all | solution.py:32
  33.4 20.5 %copy-start.2 = (bf16[1,1024,384]{2,1,0:T(8,128)(2,1)}, bf16[1,1024,384]{2,1,0:T(8,128)(2,1)S(1)}, u32[]{:S(2)}) copy-start(bf16[1,1024,384]{2,1,0:T(8,128)(2,1)S(1)} %all_gather.10) | copy-start | bytes 2359300
  43.8 10.7 %copy-start.4 = (bf16[1,1024,384]{2,1,0:T(8,128)(2,1)}, bf16[1,1024,384]{2,1,0:T(8,128)(2,1)S(1)}, u32[]{:S(2)}) copy-start(bf16[1,1024,384]{2,1,0:T(8,128)(2,1)S(1)} %all_gather.9) | copy-start | bytes 2359300
  53.2 1.3 copy-start.7
  53.8 2.2 %copy-start.9 = (f32[384,384]{0,1:T(8,128)}, f32[384,384]{0,1:T(8,128)S(1)}, u32[]{:S(2)}) copy-start(f32[384,384]{0,1:T(8,128)S(1)} %fusion.23) | copy-start | bytes 1769476
  54.5 1.5 copy-start.11
  56.0 5.2 %copy-start.13 = (bf16[128,1024]{1,0:T(8,128)(2,1)S(1)}, bf16[128,1024]{1,0:T(8,128)(2,1)}, u32[]{:S(2)}) copy-start(bf16[128,1024]{1,0:T(8,128)(2,1)} %param.12) | copy-start | bytes 786436
  56.0 25.9 %all-to-all-start.1 = ((bf16[4,96,1024]{2,1,0:T(8,128)(2,1)}), bf16[4,96,1024]{2,1,0:T(8,128)(2,1)S(1)}, u32[]{:S(2)}, u32[]{:S(2)}) async-start(bf16[4,96,1024]{2,1,0:T(8,128)(2,1)} %bitcast.55), calls=%async_computation.1 | async-start | bytes 1572864 | tf_op jit(solution)/shard_map/all_to_all | solution.py:32
  61.3 2.0 %copy-start.17 = (f32[128,2]{0,1:T(2,128)S(1)}, f32[128,2]{0,1:T(2,128)}, u32[]{:S(2)}) copy-start(f32[128,2]{0,1:T(2,128)} %param.11) | copy-start | bytes 3076
  61.3 94.8 %reduce-scatter.2.cloned.1.call-start = ((), (), s32[]{:S(2)}) async-start(), calls=%async_computation.5 | async-start | bytes 3538944 | tf_op jit(solution)/shard_map/reduce_scatter | solution.py:49
  81.9 1.2 copy-start.1
  85.5 22.5 %copy-start.8 = (bf16[1,1024,384]{2,1,0:T(8,128)(2,1)S(1)}, bf16[1,1024,384]{2,1,0:T(8,128)(2,1)}, u32[]{:S(2)}) copy-start(bf16[1,1024,384]{2,1,0:T(8,128)(2,1)} %copy-done.7) | copy-start | bytes 2359300
  85.5 22.5 %copy-start.10 = (f32[384,384]{0,1:T(8,128)S(1)}, f32[384,384]{0,1:T(8,128)}, u32[]{:S(2)}) copy-start(f32[384,384]{0,1:T(8,128)} %copy-done.9) | copy-start | bytes 1769476
  85.5 22.5 %copy-start.12 = (f32[384,384]{0,1:T(8,128)S(1)}, f32[384,384]{0,1:T(8,128)}, u32[]{:S(2)}) copy-start(f32[384,384]{0,1:T(8,128)} %copy-done.11) | copy-start | bytes 1769476
  111.4 1.1 copy-start.3
  111.4 1.4 copy-start.5
  114.5 22.7 %all-to-all-start.3 = ((bf16[4,96,1024]{2,1,0:T(8,128)(2,1)}), bf16[4,96,1024]{2,1,0:T(8,128)(2,1)S(1)}, u32[]{:S(2)}, u32[]{:S(2)}) async-start(bf16[4,96,1024]{2,1,0:T(8,128)(2,1)} %bitcast.13), calls=%async_computation.3 | async-start | bytes 1572864 | tf_op jit(solution)/shard_map/all_to_all | solution.py:32
  139.3 1.0 copy-start.6
Sparse Core Ops, SparseCore 0:
  111.6 44.3 reduce-scatter.1
where the time goes:
time: 165 us
  blocking collectives  52.5 us (32%)
  waiting for transfers between devices  46.5 us (28%)
  local copies, waits for them, and re-layouts  17.8 us (11%)
  starting transfers between devices  15.2 us (9%)
  between operations  14.3 us (9%)
  other arithmetic  10.4 us (6%)
  matrix products  7.89 us (5%)
    all_to_all x3, waiting for transfers between devices, trade_rows(): lax.all_to_all(buffer, 'expert', split_axis=0, concat_axis=0, tiled=True)  35.2 us
    all_to_all x1, blocking collectives, trade_rows(): lax.all_to_all(buffer, 'expert', split_axis=0, concat_axis=0, tiled=True)  22.3 us
    all_to_all x3, starting transfers between devices, trade_rows(): lax.all_to_all(buffer, 'expert', split_axis=0, concat_axis=0, tiled=True)  15.2 us
    reduce_scatter x1, waiting for transfers between devices, reduce_grads(): return lax.psum_scatter(piece, 'dp', scatter_dimension=0, tiled=True)  11.3 us
    all_gather x1, blocking collectives, shards(): lax.all_gather(up_weight, 'dp', axis=1, tiled=True)  10.4 us
    all_gather x1, blocking collectives, shards(): lax.all_gather(gate_weight, 'dp', axis=1, tiled=True)  10.4 us
    all_gather x1, blocking collectives, shards(): lax.all_gather(down_weight, 'dp', axis=1, tiled=True)  9.43 us
    unnamed x39, local copies, waits for them, and re-layouts  3.41 us
  transfers between devices with their start and end apart: 4, of which 3 were waited for; matrix products, arithmetic and copies ran while one was open for 8% of the time, Pallas kernels for 0%

commit v1 on v0

v1 whole, which is shorter than its diff:
```python
import functools

import jax
import jax.numpy as jnp
from jax import lax
from jax.experimental import pallas as pl
from jax.experimental.pallas import tpu as pltpu
from jax.sharding import PartitionSpec as P

BF = jnp.bfloat16
F32 = jnp.float32


def dot(a, b, ca, cb):
    return lax.dot_general(a, b, (((ca,), (cb,)), ((), ())), preferred_element_type=F32)


def layer_kernel(
    E, G, cap,
    tokens, routing, combine, upstream, gate_w, up_w, down_w,
    out, token_grad, combine_grad, gate_grad, up_grad,
    gu_full, dn_full, x_send, c_send, x_arr, c_arr, y_send, d_send, y_back, d_back,
    pres, deltas, rs_send, rs_arr, rs_own,
    row_ss, row_rs, w_ss, w_rs, g_ss, g_rs,
):
    T, D = tokens.shape
    F = gate_w.shape[2]
    shard = gate_w.shape[1]
    z = lax.axis_index("expert")
    g = lax.axis_index("dp")

    barrier = pltpu.get_barrier_semaphore()

    def greet_row(k, c):
        pl.semaphore_signal(barrier, inc=1, device_id={"expert": lax.rem(z + k, E)})
        return c

    def greet_plane(k, c):
        pl.semaphore_signal(barrier, inc=1, device_id={"dp": lax.rem(g + k, G)})
        return c

    lax.fori_loop(1, E, greet_row, 0)
    lax.fori_loop(1, G, greet_plane, 0)

    mine = pl.ds(pl.multiple_of(g * shard, shard), shard)
    gu_full[mine, pl.ds(0, F)] = gate_w[0]
    gu_full[mine, pl.ds(F, F)] = up_w[0]
    dn_full[mine, :] = down_w[0]

    r = routing[...]
    e_iota = lax.broadcasted_iota(jnp.int32, (T, E), 1)
    hit = [(r[:, k : k + 1] == e_iota) for k in range(2)]
    named = (hit[0] | hit[1]).astype(F32).astype(BF)
    before = (
        lax.broadcasted_iota(jnp.int32, (T, T), 1) < lax.broadcasted_iota(jnp.int32, (T, T), 0)
    ).astype(F32).astype(BF)
    rank = dot(before, named, 1, 0)
    s_iota = lax.broadcasted_iota(jnp.int32, (T, E * cap), 1)
    place = []
    for k in range(2):
        rank_k = jnp.sum(jnp.where(hit[k], rank, 0.0), axis=1, keepdims=True)
        slot = r[:, k : k + 1] * cap + rank_k.astype(jnp.int32)
        place.append((slot == s_iota).astype(F32).astype(BF))
    x_send[...] = dot(place[0] + place[1], tokens[...], 0, 0).astype(BF).reshape(E, cap, D)

    pl.semaphore_wait(barrier, E - 1 + G - 1)

    def row_copy(kind, k, src, dst, back=False):
        peer = lax.rem(z + k, E)
        return pltpu.make_async_remote_copy(
            src_ref=src.at[peer],
            dst_ref=dst.at[z],
            send_sem=row_ss.at[kind, k],
            recv_sem=row_rs.at[kind, k],
            device_id={"expert": peer},
        )

    def row_recv(kind, k, src, dst):
        peer = lax.rem(z + k, E)
        origin = lax.rem(z + E - k, E)
        return pltpu.make_async_remote_copy(
            src_ref=src.at[peer],
            dst_ref=dst.at[origin],
            send_sem=row_ss.at[kind, k],
            recv_sem=row_rs.at[kind, k],
            device_id={"expert": peer},
        )

    def start_rows(kind, src, dst):
        def body(k, c):
            row_copy(kind, k, src, dst).start()
            return c

        lax.fori_loop(1, E, body, 0)

    def weight_copy(part, k, ref, rows):
        peer = lax.rem(g + k, G)
        return pltpu.make_async_remote_copy(
            src_ref=ref.at[mine],
            dst_ref=ref.at[rows],
            send_sem=w_ss.at[part, k],
            recv_sem=w_rs.at[part, k],
            device_id={"dp": peer},
        )

    def start_weights(k, c):
        weight_copy(0, k, gu_full, mine).start()
        weight_copy(1, k, dn_full, mine).start()
        return c

    start_rows(0, x_send, x_arr)
    lax.fori_loop(1, G, start_weights, 0)

    uw = upstream[...].astype(F32)
    cot = [(combine[:, k : k + 1] * uw).astype(BF) for k in range(2)]
    c_all = dot(jnp.concatenate(place, axis=0), jnp.concatenate(cot, axis=0), 0, 0)
    c_send[...] = c_all.astype(BF).reshape(E, cap, D)
    start_rows(1, c_send, c_arr)
    x_arr[z] = x_send[z]
    c_arr[z] = c_send[z]

    def wait_weights(k, c):
        origin = lax.rem(g + G - k, G)
        rows = pl.ds(pl.multiple_of(origin * shard, shard), shard)
        weight_copy(0, k, gu_full, rows).wait_recv()
        weight_copy(1, k, dn_full, rows).wait_recv()
        return c

    lax.fori_loop(1, G, wait_weights, 0)

    def forward(o):
        pre = dot(x_arr[o], gu_full[...], 1, 0)
        pres[o] = pre
        gp, up = pre[:, :F], pre[:, F:]
        hidden = (gp / (1.0 + jnp.exp(-gp)) * up).astype(BF)
        return dot(hidden, dn_full[...], 1, 1).astype(BF)

    def backward(o):
        hg = dot(c_arr[o], dn_full[...], 1, 0)
        pre = pres[o]
        gp, up = pre[:, :F], pre[:, F:]
        s = 1.0 / (1.0 + jnp.exp(-gp))
        rows = pl.ds(pl.multiple_of(o * cap, cap), cap)
        deltas[rows, pl.ds(0, F)] = (hg * up * s * (1.0 + gp * (1.0 - s))).astype(BF)
        deltas[rows, pl.ds(F, F)] = (hg * (gp * s)).astype(BF)
        return dot(deltas[rows, :], gu_full[...], 1, 1).astype(BF)

    def forward_step(k, c):
        o = lax.rem(z + E - k, E)

        @pl.when(k > 0)
        def _():
            row_recv(0, k, x_send, x_arr).wait_recv()

        y_send[o] = forward(o)

        @pl.when(k > 0)
        def _():
            row_copy(2, E - k, y_send, y_back).start()

        return c

    lax.fori_loop(0, E, forward_step, 0)

    def backward_step(k, c):
        o = lax.rem(z + E - k, E)

        @pl.when(k > 0)
        def _():
            row_recv(1, k, c_send, c_arr).wait_recv()

        d_send[o] = backward(o)

        @pl.when(k > 0)
        def _():
            row_copy(3, E - k, d_send, d_back).start()

        return c

    lax.fori_loop(0, E, backward_step, 0)
    y_back[z] = y_send[z]
    d_back[z] = d_send[z]

    def grad_copy(k, dst):
        peer = lax.rem(g + k, G)
        return pltpu.make_async_remote_copy(
            src_ref=rs_send.at[peer],
            dst_ref=rs_arr.at[dst],
            send_sem=g_ss.at[k],
            recv_sem=g_rs.at[k],
            device_id={"dp": peer},
        )

    if shard % 128 == 0:

        def piece(d):
            cols = pl.ds(pl.multiple_of(d * shard, shard), shard)
            return dot(x_arr[:, :, cols].reshape(E * cap, shard), deltas[...], 0, 0)

        def grad_step(k, c):
            peer = lax.rem(g + k, G)
            rs_send[peer] = piece(peer).astype(BF)
            grad_copy(k, g).start()
            return c

        lax.fori_loop(1, G, grad_step, 0)
        rs_own[...] = piece(g)
    else:
        per = 128 // shard

        def grad_chunk(c, carry):
            cols = pl.ds(pl.multiple_of(c * 128, 128), 128)
            full = dot(x_arr[:, :, cols].reshape(E * cap, 128), deltas[...], 0, 0)
            rs_send[pl.ds(c * per, per)] = full.astype(BF).reshape(per, shard, 2 * F)
            return carry

        lax.fori_loop(0, D // 128, grad_chunk, 0)

        def grad_start(k, c):
            grad_copy(k, g).start()
            return c

        lax.fori_loop(1, G, grad_start, 0)
        rs_own[...] = rs_send[g].astype(F32)

    def wait_y(k, c):
        row_recv(2, k, y_send, y_back).wait_recv()
        return c

    lax.fori_loop(1, E, wait_y, 0)
    total = jnp.zeros((T, D), F32)
    y_all = y_back[...].reshape(E * cap, D)
    u32 = upstream[...].astype(F32)
    for k in range(2):
        picked = dot(place[k], y_all, 1, 0)
        total = total + combine[:, k : k + 1] * picked
        combine_grad[:, k : k + 1] = jnp.sum(u32 * picked, axis=1, keepdims=True)
    out[...] = total.astype(BF)

    def add_piece(k, c):
        origin = lax.rem(g + G - k, G)
        grad_copy(k, origin).wait_recv()
        rs_own[...] += rs_arr[origin].astype(F32)
        return c

    lax.fori_loop(1, G, add_piece, 0)
    gate_grad[0] = rs_own[:, pl.ds(0, F)] * (1.0 / G)
    up_grad[0] = rs_own[:, pl.ds(F, F)] * (1.0 / G)

    def wait_d(k, c):
        row_recv(3, k, d_send, d_back).wait_recv()
        return c

    lax.fori_loop(1, E, wait_d, 0)
    d_all = d_back[...].reshape(E * cap, D)
    token_grad[...] = dot(place[0] + place[1], d_all, 1, 0).astype(BF)

    def end_rows(k, c):
        row_copy(0, k, x_send, x_arr).wait_send()
        row_copy(1, k, c_send, c_arr).wait_send()
        row_copy(2, k, y_send, y_back).wait_send()
        row_copy(3, k, d_send, d_back).wait_send()
        return c

    def end_plane(k, c):
        weight_copy(0, k, gu_full, mine).wait_send()
        weight_copy(1, k, dn_full, mine).wait_send()
        grad_copy(k, g).wait_send()
        return c

    lax.fori_loop(1, E, end_rows, 0)
    lax.fori_loop(1, G, end_plane, 0)


def solution(mesh):
    E = mesh.shape["expert"]
    G = mesh.shape["dp"]

    def shards(tokens, routing, combine, upstream, gate_w, up_w, down_w):
        T, D = tokens.shape
        top = routing.shape[1]
        shard, F = gate_w.shape[1:]
        cap = max(T // 2, top * T // E + T // 4)
        rows = (E, cap, D)
        vmem = pl.BlockSpec(memory_space=pltpu.VMEM)
        return pl.pallas_call(
            functools.partial(layer_kernel, E, G, cap),
            out_shape=(
                jax.ShapeDtypeStruct((T, D), BF),
                jax.ShapeDtypeStruct((T, D), BF),
                jax.ShapeDtypeStruct((T, top), F32),
                jax.ShapeDtypeStruct((1, shard, F), F32),
                jax.ShapeDtypeStruct((1, shard, F), F32),
            ),
            in_specs=[vmem] * 7,
            out_specs=(vmem,) * 5,
            scratch_shapes=[
                pltpu.VMEM((G * shard, 2 * F), BF),
                pltpu.VMEM((G * shard, F), BF),
            ]
            + [pltpu.VMEM(rows, BF)] * 8
            + [
                pltpu.VMEM((E, cap, 2 * F), F32),
                pltpu.VMEM((E * cap, 2 * F), BF),
                pltpu.VMEM((G, shard, 2 * F), BF),
                pltpu.VMEM((G, shard, 2 * F), BF),
                pltpu.VMEM((shard, 2 * F), F32),
                pltpu.SemaphoreType.DMA((4, E)),
                pltpu.SemaphoreType.DMA((4, E)),
                pltpu.SemaphoreType.DMA((2, G)),
                pltpu.SemaphoreType.DMA((2, G)),
                pltpu.SemaphoreType.DMA((G,)),
                pltpu.SemaphoreType.DMA((G,)),
            ],
            compiler_params=pltpu.CompilerParams(
                collective_id=0, has_side_effects=True, vmem_limit_bytes=52 * 2**20
            ),
            cost_estimate=pl.CostEstimate(
                flops=16 * E * cap * D * F, bytes_accessed=8 * E * cap * D * 2, transcendentals=0
            ),
        )(tokens, routing, combine, upstream, gate_w, up_w, down_w)

    rows = P(("dp", "expert"), None)
    weights = P("expert", "dp", None)
    return jax.shard_map(
        shards,
        mesh=mesh,
        in_specs=(rows, rows, rows, rows, weights, weights, weights),
        out_specs=(rows, rows, rows, weights, weights),
        check_vma=False,
    )
```

time: 165 us -> 85.8 us (0.52)
  Pallas kernels: 0 us -> 76.1 us
  blocking collectives: 52.5 us -> 0 us
  waiting for transfers between devices: 46.5 us -> 0 us
  starting transfers between devices: 15.2 us -> 0 us
  between operations: 14.3 us -> 0.66 us
  other arithmetic: 10.4 us -> 0 us
  local copies, waits for them, and re-layouts: 17.8 us -> 8.68 us
  matrix products: 7.89 us -> 0 us
    pallas_call x0 -> x1, Pallas kernels: none -> 76.1 us  [shards(): pl.pallas_call(functools.partial(layer_kernel, E, G, cap), out_shape=(jax...]
    all_to_all x3 -> x0, waiting for transfers between devices: 35.2 us -> none  [trade_rows(): lax.all_to_all(buffer, 'expert', split_axis=0, concat_axis=0, tiled=True)]
    all_gather x3 -> x0, blocking collectives: 30.2 us -> none  [the longest x1 10.4 us: shards(): lax.all_gather(up_weight, 'dp', axis=1, tiled=True)]
    all_to_all x1 -> x0, blocking collectives: 22.3 us -> none  [trade_rows(): lax.all_to_all(buffer, 'expert', split_axis=0, concat_axis=0, tiled=True)]
    all_to_all x3 -> x0, starting transfers between devices: 15.2 us -> none  [trade_rows(): lax.all_to_all(buffer, 'expert', split_axis=0, concat_axis=0, tiled=True)]
    reduce_scatter x1 -> x0, waiting for transfers between devices: 11.3 us -> none  [reduce_grads(): return lax.psum_scatter(piece, 'dp', scatter_dimension=0, tiled=True)]
    dot_general x6 -> x0, matrix products: 7.89 us -> none  [the longest x1 2.66 us: reduce_grads(): lax.dot_general(arrived, deltas, (((0,), (0,)), ((), ())), preferred_elem...]
    gather x4 -> x0, local copies, waits for them, and re-layouts: 6.47 us -> none  [the longest x1 2.07 us: shards(): jnp.take(pick_cotangent, pick_source, axis=0, mode='fill', fill_value=0)]
  transfers between devices with their start and end apart: 4 -> 0, of which waited for: 3 -> 0; matrix products, arithmetic and copies ran while one was open for 8% -> 0% of each run, Pallas kernels for 0% -> 0%
where the time goes in v1:
time: 85.8 us; the launch traced here: 85.5 us
  Pallas kernels  76.1 us (89%)
  local copies, waits for them, and re-layouts  8.68 us (10%)
    pallas_call x1, Pallas kernels, shards(): pl.pallas_call(functools.partial(layer_kernel, E, G, cap), out_shape=(jax...  76.1 us
    unnamed x16, local copies, waits for them, and re-layouts  8.04 us

profile of v1, /device:TPU:0, one launch (start us, length us, event | category | flops | bytes accessed | tf_op | source)
XLA Modules:
  0.0 85.5 jit_solution(16082762726857088333)
XLA Ops:
  0.6 0.0 copy-start.2
  0.6 0.8 copy.12.routing
  1.5 0.8 copy.13.combine
  2.2 0.0 copy-done.2
  2.2 0.0 copy-start
  2.3 0.9 %copy-done = bf16[128,1024]{1,0:T(8,128)(2,1)S(1)} copy-done((bf16[128,1024]{1,0:T(8,128)(2,1)S(1)}, bf16[128,1024]{1,0:T(8,128)(2,1)}, u32[]{:S(2)}) %copy-start) | copy-done | bytes 262168
  3.2 0.0 copy-start.1
  3.2 0.9 %copy-done.1 = bf16[128,1024]{1,0:T(8,128)(2,1)S(1)} copy-done((bf16[128,1024]{1,0:T(8,128)(2,1)S(1)}, bf16[128,1024]{1,0:T(8,128)(2,1)}, u32[]{:S(2)}) %copy-start.1) | copy-done | bytes 262168
  4.2 0.0 copy-start.3
  4.2 0.9 %copy-done.3 = bf16[1,128,384]{2,1,0:T(8,128)(2,1)S(1)} copy-done((bf16[1,128,384]{2,1,0:T(8,128)(2,1)S(1)}, bf16[1,128,384]{2,1,0:T(8,128)(2,1)}, u32[]{:S(2)}) %copy-start.3) | copy-done | bytes 98328
  5.0 0.0 copy-start.4
  5.0 0.9 %copy-done.4 = bf16[1,128,384]{2,1,0:T(8,128)(2,1)S(1)} copy-done((bf16[1,128,384]{2,1,0:T(8,128)(2,1)S(1)}, bf16[1,128,384]{2,1,0:T(8,128)(2,1)}, u32[]{:S(2)}) %copy-start.4) | copy-done | bytes 98328
  5.9 76.1 %shard_map.110 = (bf16[128,1024]{1,0:T(8,128)(2,1)S(1)}, bf16[128,1024]{1,0:T(8,128)(2,1)S(1)}, f32[128,2]{1,0:T(8,128)S(1)}, f32[1,128,384]{2,1,0:T(8,128)S(1)}, f32[1,128,384]{2,1,0:T(8,128)S(1)}) custom-call(bf16[128,1024]{1,0:T(8,128)(2,1)S(1)} %copy-done, s32[128,2]{1,0:T(8,128)S(1)} %copy.12.routing, f32[128,2]{1,0:T(8,128)S(1)} %copy.13.combine, ...), custom_call_target="tpu_custom_call" | custom-call | flops 2415919104 | bytes 6291456 | tf_op jit(solution)/shard_map/pallas_call | solution.py:286
  82.1 0.6 copy.14
  82.7 0.7 copy.19
  83.4 0.7 copy.20
  84.1 0.7 copy.21
  84.8 0.7 copy.22
Async XLA Ops:
  0.6 1.6 %copy-start.2 = (bf16[1,128,384]{2,1,0:T(8,128)(2,1)S(1)}, bf16[1,128,384]{2,1,0:T(8,128)(2,1)}, u32[]{:S(2)}) copy-start(bf16[1,128,384]{2,1,0:T(8,128)(2,1)} %gate_w.1) | copy-start | bytes 294916
  2.2 1.0 %copy-start = (bf16[128,1024]{1,0:T(8,128)(2,1)S(1)}, bf16[128,1024]{1,0:T(8,128)(2,1)}, u32[]{:S(2)}) copy-start(bf16[128,1024]{1,0:T(8,128)(2,1)} %tokens.1) | copy-start | bytes 786436
  3.2 0.9 %copy-start.1 = (bf16[128,1024]{1,0:T(8,128)(2,1)S(1)}, bf16[128,1024]{1,0:T(8,128)(2,1)}, u32[]{:S(2)}) copy-start(bf16[128,1024]{1,0:T(8,128)(2,1)} %upstream.1) | copy-start | bytes 786436
  4.2 0.9 %copy-start.3 = (bf16[1,128,384]{2,1,0:T(8,128)(2,1)S(1)}, bf16[1,128,384]{2,1,0:T(8,128)(2,1)}, u32[]{:S(2)}) copy-start(bf16[1,128,384]{2,1,0:T(8,128)(2,1)} %up_w.1) | copy-start | bytes 294916
  5.0 0.9 %copy-start.4 = (bf16[1,128,384]{2,1,0:T(8,128)(2,1)S(1)}, bf16[1,128,384]{2,1,0:T(8,128)(2,1)}, u32[]{:S(2)}) copy-start(bf16[1,128,384]{2,1,0:T(8,128)(2,1)} %down_w.1) | copy-start | bytes 294916

commit v2 on v1

--- a/solution.py
+++ b/solution.py
@@ -17,18 +17,42 @@
 
 def layer_kernel(
     E, G, cap,
-    tokens, routing, combine, upstream, gate_w, up_w, down_w,
+    tokens_hbm, routing_rows, combine_rows, upstream_hbm, gate_w, up_w, down_w,
     out, token_grad, combine_grad, gate_grad, up_grad,
+    tokens, upstream,
     gu_full, dn_full, x_send, c_send, x_arr, c_arr, y_send, d_send, y_back, d_back,
-    pres, deltas, rs_send, rs_arr, rs_own,
-    row_ss, row_rs, w_ss, w_rs, g_ss, g_rs,
+    pres, deltas, full_grad, mate_send, mate_arr, rs_send, rs_arr, rs_own,
+    in_sem, row_ss, row_rs, w_ss, w_rs, f_ss, f_rs, m_ss, m_rs, g_ss, g_rs,
 ):
     T, D = tokens.shape
+    C = G // 2
     F = gate_w.shape[2]
     shard = gate_w.shape[1]
     z = lax.axis_index("expert")
     g = lax.axis_index("dp")
 
+    chip, core = lax.div(g, 2), lax.rem(g, 2)
+    mate = g + 1 - 2 * core
+
+    def twin(k):
+        return lax.rem(chip + k, C) * 2 + core
+
+    mine = pl.ds(pl.multiple_of(g * shard, shard), shard)
+    loads = [
+        pltpu.make_async_copy(src, dst, in_sem.at[i])
+        for i, (src, dst) in enumerate(
+            (
+                (tokens_hbm, tokens),
+                (gate_w.at[0], gu_full.at[mine, pl.ds(0, F)]),
+                (up_w.at[0], gu_full.at[mine, pl.ds(F, F)]),
+                (down_w.at[0], dn_full.at[mine]),
+                (upstream_hbm, upstream),
+            )
+        )
+    ]
+    for load in loads:
+        load.start()
+
     barrier = pltpu.get_barrier_semaphore()
 
     def greet_row(k, c):
@@ -36,18 +60,17 @@
         return c
 
     def greet_plane(k, c):
-        pl.semaphore_signal(barrier, inc=1, device_id={"dp": lax.rem(g + k, G)})
+        pl.semaphore_signal(barrier, inc=1, device_id={"dp": twin(k)})
         return c
 
     lax.fori_loop(1, E, greet_row, 0)
-    lax.fori_loop(1, G, greet_plane, 0)
-
-    mine = pl.ds(pl.multiple_of(g * shard, shard), shard)
-    gu_full[mine, pl.ds(0, F)] = gate_w[0]
-    gu_full[mine, pl.ds(F, F)] = up_w[0]
-    dn_full[mine, :] = down_w[0]
-
-    r = routing[...]
+    lax.fori_loop(1, C, greet_plane, 0)
+    pl.semaphore_signal(barrier, inc=1, device_id={"dp": mate})
+
+    both = jnp.concatenate([routing_rows[...].astype(F32), combine_rows[...]] * 2, axis=0)
+    columns = both.T
+    r = columns[:, 0:2].astype(jnp.int32)
+    combine = columns[:, 2:4]
     e_iota = lax.broadcasted_iota(jnp.int32, (T, E), 1)
     hit = [(r[:, k : k + 1] == e_iota) for k in range(2)]
     named = (hit[0] | hit[1]).astype(F32).astype(BF)
@@ -61,9 +84,10 @@
         rank_k = jnp.sum(jnp.where(hit[k], rank, 0.0), axis=1, keepdims=True)
         slot = r[:, k : k + 1] * cap + rank_k.astype(jnp.int32)
         place.append((slot == s_iota).astype(F32).astype(BF))
+    loads[0].wait()
     x_send[...] = dot(place[0] + place[1], tokens[...], 0, 0).astype(BF).reshape(E, cap, D)
 
-    pl.semaphore_wait(barrier, E - 1 + G - 1)
+    pl.semaphore_wait(barrier, E - 1 + C)
 
     def row_copy(kind, k, src, dst, back=False):
         peer = lax.rem(z + k, E)
@@ -94,14 +118,26 @@
         lax.fori_loop(1, E, body, 0)
 
     def weight_copy(part, k, ref, rows):
-        peer = lax.rem(g + k, G)
         return pltpu.make_async_remote_copy(
             src_ref=ref.at[mine],
             dst_ref=ref.at[rows],
             send_sem=w_ss.at[part, k],
             recv_sem=w_rs.at[part, k],
-            device_id={"dp": peer},
-        )
+            device_id={"dp": twin(k)},
+        )
+
+    def mate_copy(part, k, ref, rows):
+        return pltpu.make_async_remote_copy(
+            src_ref=ref.at[rows],
+            dst_ref=ref.at[rows],
+            send_sem=f_ss.at[part, k],
+            recv_sem=f_rs.at[part, k],
+            device_id={"dp": mate},
+        )
+
+    def rows_of(k, which):
+        origin = lax.rem(chip + C - k, C) * 2 + which
+        return pl.ds(pl.multiple_of(origin * shard, shard), shard)
 
     def start_weights(k, c):
         weight_copy(0, k, gu_full, mine).start()
@@ -109,24 +145,37 @@
         return c
 
     start_rows(0, x_send, x_arr)
-    lax.fori_loop(1, G, start_weights, 0)
+    for load in loads[1:]:
+        load.wait()
+    lax.fori_loop(1, C, start_weights, 0)
+    mate_copy(0, 0, gu_full, mine).start()
+    mate_copy(1, 0, dn_full, mine).start()
 
     uw = upstream[...].astype(F32)
     cot = [(combine[:, k : k + 1] * uw).astype(BF) for k in range(2)]
     c_all = dot(jnp.concatenate(place, axis=0), jnp.concatenate(cot, axis=0), 0, 0)
     c_send[...] = c_all.astype(BF).reshape(E, cap, D)
-    start_rows(1, c_send, c_arr)
     x_arr[z] = x_send[z]
     c_arr[z] = c_send[z]
 
+    def forward_weights(k, c):
+        rows = rows_of(k, core)
+        weight_copy(0, k, gu_full, rows).wait_recv()
+        mate_copy(0, k, gu_full, rows).start()
+        weight_copy(1, k, dn_full, rows).wait_recv()
+        mate_copy(1, k, dn_full, rows).start()
+        return c
+
+    lax.fori_loop(1, C, forward_weights, 0)
+    start_rows(1, c_send, c_arr)
+
     def wait_weights(k, c):
-        origin = lax.rem(g + G - k, G)
-        rows = pl.ds(pl.multiple_of(origin * shard, shard), shard)
-        weight_copy(0, k, gu_full, rows).wait_recv()
-        weight_copy(1, k, dn_full, rows).wait_recv()
-        return c
-
-    lax.fori_loop(1, G, wait_weights, 0)
+        rows = rows_of(k, 1 - core)
+        mate_copy(0, k, gu_full, rows).wait_recv()
+        mate_copy(1, k, dn_full, rows).wait_recv()
+        return c
+
+    lax.fori_loop(0, C, wait_weights, 0)
 
     def forward(o):
         pre = dot(x_arr[o], gu_full[...], 1, 0)
@@ -181,14 +230,22 @@
     y_back[z] = y_send[z]
     d_back[z] = d_send[z]
 
-    def grad_copy(k, dst):
-        peer = lax.rem(g + k, G)
-        return pltpu.make_async_remote_copy(
-            src_ref=rs_send.at[peer],
-            dst_ref=rs_arr.at[dst],
+    def mate_piece(k):
+        return pltpu.make_async_remote_copy(
+            src_ref=mate_send.at[k],
+            dst_ref=mate_arr.at[k],
+            send_sem=m_ss.at[k],
+            recv_sem=m_rs.at[k],
+            device_id={"dp": mate},
+        )
+
+    def grad_copy(k):
+        return pltpu.make_async_remote_copy(
+            src_ref=rs_send.at[k],
+            dst_ref=rs_arr.at[k],
             send_sem=g_ss.at[k],
             recv_sem=g_rs.at[k],
-            device_id={"dp": peer},
+            device_id={"dp": twin(k)},
         )
 
     if shard % 128 == 0:
@@ -197,31 +254,39 @@
             cols = pl.ds(pl.multiple_of(d * shard, shard), shard)
             return dot(x_arr[:, :, cols].reshape(E * cap, shard), deltas[...], 0, 0)
 
-        def grad_step(k, c):
-            peer = lax.rem(g + k, G)
-            rs_send[peer] = piece(peer).astype(BF)
-            grad_copy(k, g).start()
-            return c
-
-        lax.fori_loop(1, G, grad_step, 0)
-        rs_own[...] = piece(g)
     else:
         per = 128 // shard
 
         def grad_chunk(c, carry):
             cols = pl.ds(pl.multiple_of(c * 128, 128), 128)
             full = dot(x_arr[:, :, cols].reshape(E * cap, 128), deltas[...], 0, 0)
-            rs_send[pl.ds(c * per, per)] = full.astype(BF).reshape(per, shard, 2 * F)
+            full_grad[pl.ds(c * per, per)] = full.reshape(per, shard, 2 * F)
             return carry
 
         lax.fori_loop(0, D // 128, grad_chunk, 0)
 
-        def grad_start(k, c):
-            grad_copy(k, g).start()
-            return c
-
-        lax.fori_loop(1, G, grad_start, 0)
-        rs_own[...] = rs_send[g].astype(F32)
+        def piece(d):
+            return full_grad[d]
+
+    def mate_step(j, c):
+        k = lax.rem(j + 1, C)
+        mate_send[k] = piece(twin(k) + 1 - 2 * core).astype(BF)
+        mate_piece(k).start()
+        return c
+
+    lax.fori_loop(0, C, mate_step, 0)
+
+    def grad_step(k, c):
+        own = piece(twin(k))
+        mate_piece(k).wait_recv()
+        rs_send[k] = (own + mate_arr[k].astype(F32)).astype(BF)
+        grad_copy(k).start()
+        return c
+
+    lax.fori_loop(1, C, grad_step, 0)
+    own = piece(g)
+    mate_piece(0).wait_recv()
+    rs_own[...] = own + mate_arr[0].astype(F32)
 
     def wait_y(k, c):
         row_recv(2, k, y_send, y_back).wait_recv()
@@ -231,19 +296,21 @@
     total = jnp.zeros((T, D), F32)
     y_all = y_back[...].reshape(E * cap, D)
     u32 = upstream[...].astype(F32)
+    t_iota = lax.broadcasted_iota(jnp.int32, (T, T), 1)
+    sums = jnp.zeros((T, T), F32)
     for k in range(2):
         picked = dot(place[k], y_all, 1, 0)
         total = total + combine[:, k : k + 1] * picked
-        combine_grad[:, k : k + 1] = jnp.sum(u32 * picked, axis=1, keepdims=True)
+        sums = jnp.where(t_iota == k, jnp.sum(u32 * picked, axis=1, keepdims=True), sums)
+    combine_grad[...] = sums.T[:2]
     out[...] = total.astype(BF)
 
     def add_piece(k, c):
-        origin = lax.rem(g + G - k, G)
-        grad_copy(k, origin).wait_recv()
-        rs_own[...] += rs_arr[origin].astype(F32)
-        return c
-
-    lax.fori_loop(1, G, add_piece, 0)
+        grad_copy(k).wait_recv()
+        rs_own[...] += rs_arr[k].astype(F32)
+        return c
+
+    lax.fori_loop(1, C, add_piece, 0)
     gate_grad[0] = rs_own[:, pl.ds(0, F)] * (1.0 / G)
     up_grad[0] = rs_own[:, pl.ds(F, F)] * (1.0 / G)
 
@@ -262,14 +329,21 @@
         row_copy(3, k, d_send, d_back).wait_send()
         return c
 
+    def end_mate(k, c):
+        mate_copy(0, k, gu_full, mine).wait_send()
+        mate_copy(1, k, dn_full, mine).wait_send()
+        mate_piece(k).wait_send()
+        return c
+
     def end_plane(k, c):
         weight_copy(0, k, gu_full, mine).wait_send()
         weight_copy(1, k, dn_full, mine).wait_send()
-        grad_copy(k, g).wait_send()
+        grad_copy(k).wait_send()
         return c
 
     lax.fori_loop(1, E, end_rows, 0)
-    lax.fori_loop(1, G, end_plane, 0)
+    lax.fori_loop(0, C, end_mate, 0)
+    lax.fori_loop(1, C, end_plane, 0)
 
 
 def solution(mesh):
@@ -283,18 +357,21 @@
         cap = max(T // 2, top * T // E + T // 4)
         rows = (E, cap, D)
         vmem = pl.BlockSpec(memory_space=pltpu.VMEM)
-        return pl.pallas_call(
+        hbm = pl.BlockSpec(memory_space=pltpu.HBM)
+        results = pl.pallas_call(
             functools.partial(layer_kernel, E, G, cap),
             out_shape=(
                 jax.ShapeDtypeStruct((T, D), BF),
                 jax.ShapeDtypeStruct((T, D), BF),
-                jax.ShapeDtypeStruct((T, top), F32),
+                jax.ShapeDtypeStruct((top, T), F32),
                 jax.ShapeDtypeStruct((1, shard, F), F32),
                 jax.ShapeDtypeStruct((1, shard, F), F32),
             ),
-            in_specs=[vmem] * 7,
+            in_specs=[hbm, vmem, vmem, hbm, hbm, hbm, hbm],
             out_specs=(vmem,) * 5,
             scratch_shapes=[
+                pltpu.VMEM((T, D), BF),
+                pltpu.VMEM((T, D), BF),
                 pltpu.VMEM((G * shard, 2 * F), BF),
                 pltpu.VMEM((G * shard, F), BF),
             ]
@@ -302,23 +379,25 @@
             + [
                 pltpu.VMEM((E, cap, 2 * F), F32),
                 pltpu.VMEM((E * cap, 2 * F), BF),
-                pltpu.VMEM((G, shard, 2 * F), BF),
-                pltpu.VMEM((G, shard, 2 * F), BF),
+                pltpu.VMEM((G, shard, 2 * F), F32),
+            ]
+            + [pltpu.VMEM((G // 2, shard, 2 * F), BF)] * 4
+            + [
                 pltpu.VMEM((shard, 2 * F), F32),
+                pltpu.SemaphoreType.DMA((5,)),
                 pltpu.SemaphoreType.DMA((4, E)),
                 pltpu.SemaphoreType.DMA((4, E)),
-                pltpu.SemaphoreType.DMA((2, G)),
-                pltpu.SemaphoreType.DMA((2, G)),
-                pltpu.SemaphoreType.DMA((G,)),
-                pltpu.SemaphoreType.DMA((G,)),
-            ],
+            ]
+            + [pltpu.SemaphoreType.DMA((2, G // 2))] * 4
+            + [pltpu.SemaphoreType.DMA((G // 2,))] * 4,
             compiler_params=pltpu.CompilerParams(
-                collective_id=0, has_side_effects=True, vmem_limit_bytes=52 * 2**20
+                collective_id=0, has_side_effects=True, vmem_limit_bytes=63 * 2**20
             ),
             cost_estimate=pl.CostEstimate(
                 flops=16 * E * cap * D * F, bytes_accessed=8 * E * cap * D * 2, transcendentals=0
             ),
-        )(tokens, routing, combine, upstream, gate_w, up_w, down_w)
+        )(tokens, routing.T, combine.T, upstream, gate_w, up_w, down_w)
+        return (results[0], results[1], results[2].T, results[3], results[4])
 
     rows = P(("dp", "expert"), None)
     weights = P("expert", "dp", None)

time: 85.8 us -> 82.7 us (0.964)
  local copies, waits for them, and re-layouts: 8.68 us -> 4.66 us
  Pallas kernels: 76.1 us -> 77.2 us
    unnamed x16 -> x13, local copies, waits for them, and re-layouts: 8.04 us -> 4.66 us
    pallas_call x1, Pallas kernels: 76.1 us -> 77.2 us  [shards(): pl.pallas_call(functools.partial(layer_kernel, E, G, cap), out_shape=(jax...]
where the time goes in v2:
time: 82.7 us; the launch traced here: 82.5 us
  Pallas kernels  77.2 us (93%)
  local copies, waits for them, and re-layouts  4.66 us (6%)
    pallas_call x1, Pallas kernels, shards(): pl.pallas_call(functools.partial(layer_kernel, E, G, cap), out_shape=(jax...  77.2 us
    unnamed x13, local copies, waits for them, and re-layouts  4.66 us

profile of v2, /device:TPU:0, one launch (start us, length us, event | category | flops | bytes accessed | tf_op | source)
XLA Modules:
  0.0 82.5 jit_solution(9873677313330334642)
XLA Ops:
  0.6 77.2 %shard_map.110 = (bf16[128,1024]{1,0:T(8,128)(2,1)}, bf16[128,1024]{1,0:T(8,128)(2,1)}, f32[2,128]{1,0:T(2,128)}, f32[1,128,384]{2,1,0:T(8,128)}, f32[1,128,384]{2,1,0:T(8,128)}) custom-call(bf16[128,1024]{1,0:T(8,128)(2,1)} %tokens_hbm.1, s32[2,128]{1,0:T(2,128)} %bitcast.4, f32[2,128]{1,0:T(2,128)} %bitcast.5, bf16[128,1024]{1,0:T(8,128)(2,1)} %upstream_hbm.1, ...), custom_call_target="tpu_custom_call" | custom-call | flops 2415919104 | bytes 6291456 | tf_op jit(solution)/shard_map/pallas_call | solution.py:361
  77.8 0.0 copy-start
  77.9 1.7 %copy.17 = bf16[128,1024]{1,0:T(8,128)(2,1)} copy(bf16[128,1024]{1,0:T(8,128)(2,1)} %get-tuple-element.20) | data formatting | bytes 524288
  79.6 0.0 copy-done
  79.6 0.0 copy-start.3
  79.6 0.0 copy-start.2
  79.6 0.7 copy.18
  80.3 0.0 copy-done.3
  80.3 0.6 copy.19
  80.8 0.0 copy-done.2
  80.8 0.0 copy-start.1
  80.8 0.7 copy.20
  81.5 0.3 copy-done.1
  81.8 0.7 copy.21
Async XLA Ops:
  77.8 1.7 %copy-start = (bf16[128,1024]{1,0:T(8,128)(2,1)S(1)}, bf16[128,1024]{1,0:T(8,128)(2,1)}, u32[]{:S(2)}) copy-start(bf16[128,1024]{1,0:T(8,128)(2,1)} %get-tuple-element.21) | copy-start | bytes 786436
  79.6 0.7 copy-start.3
  79.6 1.3 %copy-start.2 = (f32[1,128,384]{2,1,0:T(8,128)S(1)}, f32[1,128,384]{2,1,0:T(8,128)}, u32[]{:S(2)}) copy-start(f32[1,128,384]{2,1,0:T(8,128)} %get-tuple-element.23) | copy-start | bytes 589828
  80.8 1.0 %copy-start.1 = (f32[1,128,384]{2,1,0:T(8,128)S(1)}, f32[1,128,384]{2,1,0:T(8,128)}, u32[]{:S(2)}) copy-start(f32[1,128,384]{2,1,0:T(8,128)} %get-tuple-element.24) | copy-start | bytes 589828

commit v3 on v2

--- a/solution.py
+++ b/solution.py
@@ -19,13 +19,15 @@
     E, G, cap,
     tokens_hbm, routing_rows, combine_rows, upstream_hbm, gate_w, up_w, down_w,
     out, token_grad, combine_grad, gate_grad, up_grad,
-    tokens, upstream,
+    tokens, upstream, info, info_arr, block_arr, relay_send,
     gu_full, dn_full, x_send, c_send, x_arr, c_arr, y_send, d_send, y_back, d_back,
     pres, deltas, full_grad, mate_send, mate_arr, rs_send, rs_arr, rs_own,
     in_sem, row_ss, row_rs, w_ss, w_rs, f_ss, f_rs, m_ss, m_rs, g_ss, g_rs,
+    b_ss, b_rs, r_ss, r_rs,
 ):
     T, D = tokens.shape
     C = G // 2
+    relayed = E == 4
     F = gate_w.shape[2]
     shard = gate_w.shape[1]
     z = lax.axis_index("expert")
@@ -68,22 +70,30 @@
     pl.semaphore_signal(barrier, inc=1, device_id={"dp": mate})
 
     both = jnp.concatenate([routing_rows[...].astype(F32), combine_rows[...]] * 2, axis=0)
-    columns = both.T
-    r = columns[:, 0:2].astype(jnp.int32)
-    combine = columns[:, 2:4]
-    e_iota = lax.broadcasted_iota(jnp.int32, (T, E), 1)
-    hit = [(r[:, k : k + 1] == e_iota) for k in range(2)]
-    named = (hit[0] | hit[1]).astype(F32).astype(BF)
-    before = (
-        lax.broadcasted_iota(jnp.int32, (T, T), 1) < lax.broadcasted_iota(jnp.int32, (T, T), 0)
-    ).astype(F32).astype(BF)
-    rank = dot(before, named, 1, 0)
-    s_iota = lax.broadcasted_iota(jnp.int32, (T, E * cap), 1)
-    place = []
-    for k in range(2):
-        rank_k = jnp.sum(jnp.where(hit[k], rank, 0.0), axis=1, keepdims=True)
-        slot = r[:, k : k + 1] * cap + rank_k.astype(jnp.int32)
-        place.append((slot == s_iota).astype(F32).astype(BF))
+    info[...] = both
+
+    def picks_of(rows):
+        columns = rows.T
+        ids = columns[:, 0:2].astype(jnp.int32)
+        e_iota = lax.broadcasted_iota(jnp.int32, (T, E), 1)
+        hit = [(ids[:, k : k + 1] == e_iota) for k in range(2)]
+        named = (hit[0] | hit[1]).astype(F32).astype(BF)
+        before = (
+            lax.broadcasted_iota(jnp.int32, (T, T), 1) < lax.broadcasted_iota(jnp.int32, (T, T), 0)
+        ).astype(F32).astype(BF)
+        rank = dot(before, named, 1, 0)
+        slots = []
+        for k in range(2):
+            rank_k = jnp.sum(jnp.where(hit[k], rank, 0.0), axis=1, keepdims=True)
+            slots.append(ids[:, k : k + 1] * cap + rank_k.astype(jnp.int32))
+        return slots, columns[:, 2:4]
+
+    def places(slots, width, first):
+        s_iota = lax.broadcasted_iota(jnp.int32, (T, width), 1) + first
+        return [(slot == s_iota).astype(F32).astype(BF) for slot in slots]
+
+    slots, combine = picks_of(both)
+    place = places(slots, E * cap, 0)
     loads[0].wait()
     x_send[...] = dot(place[0] + place[1], tokens[...], 0, 0).astype(BF).reshape(E, cap, D)
 
@@ -144,7 +154,91 @@
         weight_copy(1, k, dn_full, mine).start()
         return c
 
-    start_rows(0, x_send, x_arr)
+    half = lax.div(z, 2)
+    near = 2 - half
+    partner = z + 1 - 2 * lax.rem(z, 2)
+    boundary = (z == 1) | (z == 2)
+
+    def info_copy(k, slot):
+        return pltpu.make_async_remote_copy(
+            src_ref=info,
+            dst_ref=info_arr.at[slot],
+            send_sem=row_ss.at[4, k],
+            recv_sem=row_rs.at[4, k],
+            device_id={"expert": lax.rem(z + k, E)},
+        )
+
+    def block_copy(kind, src, i):
+        return pltpu.make_async_remote_copy(
+            src_ref=src,
+            dst_ref=block_arr.at[kind, i],
+            send_sem=b_ss.at[kind],
+            recv_sem=b_rs.at[kind, i],
+            device_id={"expert": near},
+        )
+
+    def partner_copy(kind, src, dst, slot):
+        return pltpu.make_async_remote_copy(
+            src_ref=src.at[partner],
+            dst_ref=dst.at[slot],
+            send_sem=row_ss.at[kind, 1],
+            recv_sem=row_rs.at[kind, 1],
+            device_id={"expert": partner},
+        )
+
+    def relay_copy(kind, i, dst):
+        return pltpu.make_async_remote_copy(
+            src_ref=relay_send.at[kind, i],
+            dst_ref=dst.at[2 * (1 - half) + i],
+            send_sem=r_ss.at[kind, i],
+            recv_sem=r_rs.at[kind, i],
+            device_id={"expert": partner},
+        )
+
+    def near_first(j):
+        return half * (1 - j) + (1 - half) * j
+
+    def relay(kind, dst):
+        @pl.when(boundary)
+        def _():
+            def body(j, c):
+                i = near_first(j)
+                o = 2 * (1 - half) + i
+                block_copy(kind, tokens, i).wait_recv()
+                slots_o, combine_o = picks_of(info_arr[o])
+                block = block_arr[kind, i]
+                if kind == 1:
+                    wide = block.astype(F32)
+                    block = jnp.concatenate(
+                        [(combine_o[:, k : k + 1] * wide).astype(BF) for k in range(2)], axis=0
+                    )
+
+                def chosen(e):
+                    found = places(slots_o, cap, e * cap)
+                    found = found[0] + found[1] if kind == 0 else jnp.concatenate(found, axis=0)
+                    return dot(found, block, 0, 0).astype(BF)
+
+                relay_send[kind, i] = chosen(partner)
+                relay_copy(kind, i, dst).start()
+                dst[o] = chosen(z)
+                return c
+
+            lax.fori_loop(0, 2, body, 0)
+
+    def start_info(k, c):
+        info_copy(k, z).start()
+        return c
+
+    def wait_info(k, c):
+        info_copy(k, lax.rem(z + E - k, E)).wait_recv()
+        return c
+
+    if relayed:
+        lax.fori_loop(1, E, start_info, 0)
+        block_copy(0, tokens, lax.rem(z, 2)).start()
+        partner_copy(0, x_send, x_arr, z).start()
+    else:
+        start_rows(0, x_send, x_arr)
     for load in loads[1:]:
         load.wait()
     lax.fori_loop(1, C, start_weights, 0)
@@ -167,7 +261,13 @@
         return c
 
     lax.fori_loop(1, C, forward_weights, 0)
-    start_rows(1, c_send, c_arr)
+    if relayed:
+        block_copy(1, upstream, lax.rem(z, 2)).start()
+        partner_copy(1, c_send, c_arr, z).start()
+        lax.fori_loop(1, E, wait_info, 0)
+        relay(0, x_arr)
+    else:
+        start_rows(1, c_send, c_arr)
 
     def wait_weights(k, c):
         rows = rows_of(k, 1 - core)
@@ -194,38 +294,50 @@
         deltas[rows, pl.ds(F, F)] = (hg * (gp * s)).astype(BF)
         return dot(deltas[rows, :], gu_full[...], 1, 1).astype(BF)
 
-    def forward_step(k, c):
-        o = lax.rem(z + E - k, E)
+    def origin_of(k):
+        if not relayed:
+            return lax.rem(z + E - k, E)
+        other = 2 * (1 - half) + near_first(lax.rem(k, 2))
+        return jnp.where(k == 0, z, jnp.where(k == 1, partner, other))
+
+    def step(kind, k, src, dst, work, sent, back):
+        o = origin_of(k)
+        if relayed:
+
+            @pl.when(k == 1)
+            def _():
+                partner_copy(kind, src, dst, partner).wait_recv()
+
+            @pl.when((k > 1) & jnp.logical_not(boundary))
+            def _():
+                relay_copy(kind, near_first(lax.rem(k, 2)), dst).wait_recv()
+
+        else:
+
+            @pl.when(k > 0)
+            def _():
+                row_recv(kind, k, src, dst).wait_recv()
+
+        sent[o] = work(o)
 
         @pl.when(k > 0)
         def _():
-            row_recv(0, k, x_send, x_arr).wait_recv()
-
-        y_send[o] = forward(o)
-
-        @pl.when(k > 0)
-        def _():
-            row_copy(2, E - k, y_send, y_back).start()
-
-        return c
-
-    lax.fori_loop(0, E, forward_step, 0)
+            row_copy(kind + 2, lax.rem(o - z + E, E), sent, back).start()
+
+    def forward_step(k, c):
+        step(0, k, x_send, x_arr, forward, y_send, y_back)
+        return c
 
     def backward_step(k, c):
-        o = lax.rem(z + E - k, E)
-
-        @pl.when(k > 0)
-        def _():
-            row_recv(1, k, c_send, c_arr).wait_recv()
-
-        d_send[o] = backward(o)
-
-        @pl.when(k > 0)
-        def _():
-            row_copy(3, E - k, d_send, d_back).start()
-
-        return c
-
+        step(1, k, c_send, c_arr, backward, d_send, d_back)
+        return c
+
+    if relayed:
+        lax.fori_loop(0, 2, forward_step, 0)
+        relay(1, c_arr)
+        lax.fori_loop(2, E, forward_step, 0)
+    else:
+        lax.fori_loop(0, E, forward_step, 0)
     lax.fori_loop(0, E, backward_step, 0)
     y_back[z] = y_send[z]
     d_back[z] = d_send[z]
@@ -323,8 +435,11 @@
     token_grad[...] = dot(place[0] + place[1], d_all, 1, 0).astype(BF)
 
     def end_rows(k, c):
-        row_copy(0, k, x_send, x_arr).wait_send()
-        row_copy(1, k, c_send, c_arr).wait_send()
+        if relayed:
+            info_copy(k, z).wait_send()
+        else:
+            row_copy(0, k, x_send, x_arr).wait_send()
+            row_copy(1, k, c_send, c_arr).wait_send()
         row_copy(2, k, y_send, y_back).wait_send()
         row_copy(3, k, d_send, d_back).wait_send()
         return c
@@ -342,6 +457,16 @@
         return c
 
     lax.fori_loop(1, E, end_rows, 0)
+    if relayed:
+        for kind, block, rows, dst in ((0, tokens, x_send, x_arr), (1, upstream, c_send, c_arr)):
+            block_copy(kind, block, 0).wait_send()
+            partner_copy(kind, rows, dst, z).wait_send()
+
+            @pl.when(boundary)
+            def _():
+                relay_copy(kind, 0, dst).wait_send()
+                relay_copy(kind, 1, dst).wait_send()
+
     lax.fori_loop(0, C, end_mate, 0)
     lax.fori_loop(1, C, end_plane, 0)
 
@@ -372,6 +497,10 @@
             scratch_shapes=[
                 pltpu.VMEM((T, D), BF),
                 pltpu.VMEM((T, D), BF),
+                pltpu.VMEM((4 * top, T), F32),
+                pltpu.VMEM((E, 4 * top, T), F32),
+                pltpu.VMEM((2, 2, T, D), BF),
+                pltpu.VMEM((2, 2, cap, D), BF),
                 pltpu.VMEM((G * shard, 2 * F), BF),
                 pltpu.VMEM((G * shard, F), BF),
             ]
@@ -385,11 +514,13 @@
             + [
                 pltpu.VMEM((shard, 2 * F), F32),
                 pltpu.SemaphoreType.DMA((5,)),
-                pltpu.SemaphoreType.DMA((4, E)),
-                pltpu.SemaphoreType.DMA((4, E)),
+                pltpu.SemaphoreType.DMA((5, E)),
+                pltpu.SemaphoreType.DMA((5, E)),
             ]
             + [pltpu.SemaphoreType.DMA((2, G // 2))] * 4
-            + [pltpu.SemaphoreType.DMA((G // 2,))] * 4,
+            + [pltpu.SemaphoreType.DMA((G // 2,))] * 4
+            + [pltpu.SemaphoreType.DMA((2,))]
+            + [pltpu.SemaphoreType.DMA((2, 2))] * 3,
             compiler_params=pltpu.CompilerParams(
                 collective_id=0, has_side_effects=True, vmem_limit_bytes=63 * 2**20
             ),

time: 82.7 us -> 77.7 us (0.940)
  Pallas kernels: 77.2 us -> 72.2 us
    pallas_call x1, Pallas kernels: 77.2 us -> 72.2 us  [shards(): pl.pallas_call(functools.partial(layer_kernel, E, G, cap), out_shape=(jax...]
where the time goes in v3:
time: 77.7 us; the launch traced here: 77.5 us
  Pallas kernels  72.2 us (93%)
  local copies, waits for them, and re-layouts  4.66 us (6%)
    pallas_call x1, Pallas kernels, shards(): pl.pallas_call(functools.partial(layer_kernel, E, G, cap), out_shape=(jax...  72.2 us
    unnamed x13, local copies, waits for them, and re-layouts  4.66 us

profile of v3, /device:TPU:0, one launch (start us, length us, event | category | flops | bytes accessed | tf_op | source)
XLA Modules:
  0.0 77.5 jit_solution(15554819037023398995)
XLA Ops:
  0.6 72.2 %shard_map.110 = (bf16[128,1024]{1,0:T(8,128)(2,1)}, bf16[128,1024]{1,0:T(8,128)(2,1)}, f32[2,128]{1,0:T(2,128)}, f32[1,128,384]{2,1,0:T(8,128)}, f32[1,128,384]{2,1,0:T(8,128)}) custom-call(bf16[128,1024]{1,0:T(8,128)(2,1)} %tokens_hbm.1, s32[2,128]{1,0:T(2,128)} %bitcast.4, f32[2,128]{1,0:T(2,128)} %bitcast.5, bf16[128,1024]{1,0:T(8,128)(2,1)} %upstream_hbm.1, ...), custom_call_target="tpu_custom_call" | custom-call | flops 2415919104 | bytes 6291456 | tf_op jit(solution)/shard_map/pallas_call | solution.py:486
  72.9 0.0 copy-start
  72.9 1.7 %copy.17 = bf16[128,1024]{1,0:T(8,128)(2,1)} copy(bf16[128,1024]{1,0:T(8,128)(2,1)} %get-tuple-element.20) | data formatting | bytes 524288
  74.6 0.0 copy-done
  74.6 0.0 copy-start.3
  74.6 0.0 copy-start.2
  74.6 0.7 copy.18
  75.3 0.0 copy-done.3
  75.3 0.6 copy.19
  75.9 0.0 copy-done.2
  75.9 0.0 copy-start.1
  75.9 0.7 copy.20
  76.5 0.3 copy-done.1
  76.9 0.7 copy.21
Async XLA Ops:
  72.9 1.7 %copy-start = (bf16[128,1024]{1,0:T(8,128)(2,1)S(1)}, bf16[128,1024]{1,0:T(8,128)(2,1)}, u32[]{:S(2)}) copy-start(bf16[128,1024]{1,0:T(8,128)(2,1)} %get-tuple-element.21) | copy-start | bytes 786436
  74.6 0.7 copy-start.3
  74.6 1.3 %copy-start.2 = (f32[1,128,384]{2,1,0:T(8,128)S(1)}, f32[1,128,384]{2,1,0:T(8,128)}, u32[]{:S(2)}) copy-start(f32[1,128,384]{2,1,0:T(8,128)} %get-tuple-element.23) | copy-start | bytes 589828
  75.9 1.0 %copy-start.1 = (f32[1,128,384]{2,1,0:T(8,128)S(1)}, f32[1,128,384]{2,1,0:T(8,128)}, u32[]{:S(2)}) copy-start(f32[1,128,384]{2,1,0:T(8,128)} %get-tuple-element.24) | copy-start | bytes 589828

commit v4 on v3

--- a/solution.py
+++ b/solution.py
@@ -19,11 +19,11 @@
     E, G, cap,
     tokens_hbm, routing_rows, combine_rows, upstream_hbm, gate_w, up_w, down_w,
     out, token_grad, combine_grad, gate_grad, up_grad,
-    tokens, upstream, info, info_arr, block_arr, relay_send,
+    tokens, upstream, info, info_arr, block_arr, relay_send, end_back, part_send, part_arr,
     gu_full, dn_full, x_send, c_send, x_arr, c_arr, y_send, d_send, y_back, d_back,
     pres, deltas, full_grad, mate_send, mate_arr, rs_send, rs_arr, rs_own,
     in_sem, row_ss, row_rs, w_ss, w_rs, f_ss, f_rs, m_ss, m_rs, g_ss, g_rs,
-    b_ss, b_rs, r_ss, r_rs,
+    b_ss, b_rs, r_ss, r_rs, e_ss, e_rs, p_ss, p_rs,
 ):
     T, D = tokens.shape
     C = G // 2
@@ -195,6 +195,24 @@
             device_id={"expert": partner},
         )
 
+    def end_copy(i):
+        return pltpu.make_async_remote_copy(
+            src_ref=d_send.at[2 * (1 - half) + i],
+            dst_ref=end_back.at[i],
+            send_sem=e_ss.at[i],
+            recv_sem=e_rs.at[i],
+            device_id={"expert": partner},
+        )
+
+    def part_copy(i):
+        return pltpu.make_async_remote_copy(
+            src_ref=part_send.at[i],
+            dst_ref=part_arr,
+            send_sem=p_ss.at[i],
+            recv_sem=p_rs.at[0],
+            device_id={"expert": 2 * (1 - half) + i},
+        )
+
     def near_first(j):
         return half * (1 - j) + (1 - half) * j
 
@@ -320,9 +338,17 @@
 
         sent[o] = work(o)
 
-        @pl.when(k > 0)
+        summed = relayed and kind == 1
+
+        @pl.when((k == 1) if summed else (k > 0))
         def _():
             row_copy(kind + 2, lax.rem(o - z + E, E), sent, back).start()
+
+        if summed:
+
+            @pl.when((k > 1) & jnp.logical_not(boundary))
+            def _():
+                end_copy(near_first(lax.rem(k, 2))).start()
 
     def forward_step(k, c):
         step(0, k, x_send, x_arr, forward, y_send, y_back)
@@ -339,6 +365,28 @@
     else:
         lax.fori_loop(0, E, forward_step, 0)
     lax.fori_loop(0, E, backward_step, 0)
+
+    if relayed:
+        d_back[2 * (1 - half)] = jnp.zeros((cap, D), BF)
+        d_back[2 * (1 - half) + 1] = jnp.zeros((cap, D), BF)
+
+        @pl.when(boundary)
+        def _():
+            def body(j, c):
+                i = near_first(j)
+                o = 2 * (1 - half) + i
+                slots_o, _ = picks_of(info_arr[o])
+                found = places(slots_o, cap, z * cap)
+                sums = dot(found[0] + found[1], d_send[o], 1, 0)
+                found = places(slots_o, cap, partner * cap)
+                end_copy(i).wait_recv()
+                sums = sums + dot(found[0] + found[1], end_back[i], 1, 0)
+                part_send[i] = sums.astype(BF)
+                part_copy(i).start()
+                return c
+
+            lax.fori_loop(0, 2, body, 0)
+
     y_back[z] = y_send[z]
     d_back[z] = d_send[z]
 
@@ -430,9 +478,16 @@
         row_recv(3, k, d_send, d_back).wait_recv()
         return c
 
-    lax.fori_loop(1, E, wait_d, 0)
+    if relayed:
+        wait_d(lax.rem(z - partner + E, E), 0)
+        part_copy(0).wait_recv()
+    else:
+        lax.fori_loop(1, E, wait_d, 0)
     d_all = d_back[...].reshape(E * cap, D)
-    token_grad[...] = dot(place[0] + place[1], d_all, 1, 0).astype(BF)
+    sums = dot(place[0] + place[1], d_all, 1, 0)
+    if relayed:
+        sums = sums + part_arr[...].astype(F32)
+    token_grad[...] = sums.astype(BF)
 
     def end_rows(k, c):
         if relayed:
@@ -441,7 +496,8 @@
             row_copy(0, k, x_send, x_arr).wait_send()
             row_copy(1, k, c_send, c_arr).wait_send()
         row_copy(2, k, y_send, y_back).wait_send()
-        row_copy(3, k, d_send, d_back).wait_send()
+        if not relayed:
+            row_copy(3, k, d_send, d_back).wait_send()
         return c
 
     def end_mate(k, c):
@@ -458,6 +514,18 @@
 
     lax.fori_loop(1, E, end_rows, 0)
     if relayed:
+        row_copy(3, lax.rem(partner - z + E, E), d_send, d_back).wait_send()
+
+        @pl.when(boundary)
+        def _():
+            part_copy(0).wait_send()
+            part_copy(1).wait_send()
+
+        @pl.when(jnp.logical_not(boundary))
+        def _():
+            end_copy(0).wait_send()
+            end_copy(1).wait_send()
+
         for kind, block, rows, dst in ((0, tokens, x_send, x_arr), (1, upstream, c_send, c_arr)):
             block_copy(kind, block, 0).wait_send()
             partner_copy(kind, rows, dst, z).wait_send()
@@ -501,6 +569,9 @@
                 pltpu.VMEM((E, 4 * top, T), F32),
                 pltpu.VMEM((2, 2, T, D), BF),
                 pltpu.VMEM((2, 2, cap, D), BF),
+                pltpu.VMEM((2, cap, D), BF),
+                pltpu.VMEM((2, T, D), BF),
+                pltpu.VMEM((T, D), BF),
                 pltpu.VMEM((G * shard, 2 * F), BF),
                 pltpu.VMEM((G * shard, F), BF),
             ]
@@ -520,7 +591,8 @@
             + [pltpu.SemaphoreType.DMA((2, G // 2))] * 4
             + [pltpu.SemaphoreType.DMA((G // 2,))] * 4
             + [pltpu.SemaphoreType.DMA((2,))]
-            + [pltpu.SemaphoreType.DMA((2, 2))] * 3,
+            + [pltpu.SemaphoreType.DMA((2, 2))] * 3
+            + [pltpu.SemaphoreType.DMA((2,))] * 4,
             compiler_params=pltpu.CompilerParams(
                 collective_id=0, has_side_effects=True, vmem_limit_bytes=63 * 2**20
             ),

time: 77.7 us -> 81 us (1.042)
  the two profiles are of different devices: /device:TPU:0 before, /device:TPU:9 now
where the time goes in v4:
time: 81 us; the launch traced here: 80.8 us
  Pallas kernels  75.5 us (93%)
  local copies, waits for them, and re-layouts  4.66 us (6%)
    pallas_call x1, Pallas kernels, shards(): pl.pallas_call(functools.partial(layer_kernel, E, G, cap), out_shape=(jax...  75.5 us
    unnamed x13, local copies, waits for them, and re-layouts  4.66 us

profile of v4, /device:TPU:9, one launch (start us, length us, event | category | flops | bytes accessed | tf_op | source)
XLA Modules:
  0.0 80.8 jit_solution(7230621591912175598)
XLA Ops:
  0.6 75.5 %shard_map.110 = (bf16[128,1024]{1,0:T(8,128)(2,1)}, bf16[128,1024]{1,0:T(8,128)(2,1)}, f32[2,128]{1,0:T(2,128)}, f32[1,128,384]{2,1,0:T(8,128)}, f32[1,128,384]{2,1,0:T(8,128)}) custom-call(bf16[128,1024]{1,0:T(8,128)(2,1)} %tokens_hbm.1, s32[2,128]{1,0:T(2,128)} %bitcast.4, f32[2,128]{1,0:T(2,128)} %bitcast.5, bf16[128,1024]{1,0:T(8,128)(2,1)} %upstream_hbm.1, ...), custom_call_target="tpu_custom_call" | custom-call | flops 2415919104 | bytes 6291456 | tf_op jit(solution)/shard_map/pallas_call | solution.py:554
  76.1 0.0 copy-start
  76.1 1.7 %copy.17 = bf16[128,1024]{1,0:T(8,128)(2,1)} copy(bf16[128,1024]{1,0:T(8,128)(2,1)} %get-tuple-element.20) | data formatting | bytes 524288
  77.9 0.0 copy-done
  77.9 0.0 copy-start.3
  77.9 0.0 copy-start.2
  77.9 0.7 copy.18
  78.6 0.0 copy-done.3
  78.6 0.6 copy.19
  79.1 0.0 copy-done.2
  79.1 0.0 copy-start.1
  79.1 0.7 copy.20
  79.8 0.3 copy-done.1
  80.1 0.7 copy.21
Async XLA Ops:
  76.1 1.7 %copy-start = (bf16[128,1024]{1,0:T(8,128)(2,1)S(1)}, bf16[128,1024]{1,0:T(8,128)(2,1)}, u32[]{:S(2)}) copy-start(bf16[128,1024]{1,0:T(8,128)(2,1)} %get-tuple-element.21) | copy-start | bytes 786436
  77.9 0.7 copy-start.3
  77.9 1.3 %copy-start.2 = (f32[1,128,384]{2,1,0:T(8,128)S(1)}, f32[1,128,384]{2,1,0:T(8,128)}, u32[]{:S(2)}) copy-start(f32[1,128,384]{2,1,0:T(8,128)} %get-tuple-element.23) | copy-start | bytes 589828
  79.1 1.0 %copy-start.1 = (f32[1,128,384]{2,1,0:T(8,128)S(1)}, f32[1,128,384]{2,1,0:T(8,128)}, u32[]{:S(2)}) copy-start(f32[1,128,384]{2,1,0:T(8,128)} %get-tuple-element.24) | copy-start | bytes 589828
